TPU v7x, 32 devices: a whole 2x2x4 slice. The times are simulated.
32 devices in a mesh: seq: 8 (over z, y), grp: 4 (over x, core).
Axes of the slice: x: 2, y: 2, z: 4, core: 2. Of those that a mesh axis runs over, the one named last changes fastest.
Arguments:
- query: bfloat16 [4, 1024, 2048], P('grp', 'seq'), may hold values from -6 to 6
- key_in: bfloat16 [4, 1024, 2048], P('grp', 'seq'), may hold values from -6 to 6
- value: bfloat16 [4, 1024, 2048], P('grp', 'seq'), may hold values from -6 to 6
- cotangent: bfloat16 [4, 1024, 2048], P('grp', 'seq'), may hold values from -6 to 6
- routes: int32 [4, 1024, 6], P('grp', 'seq'), may hold values from 0 to 15, as said below
- gates: float32 [4, 1024, 6], P('grp', 'seq'), may hold values from 0.01 to 0.1
- hidden: bfloat16 [4, 1024, 6, 704], P('grp', 'seq'), may hold values from -6 to 6
Outputs:
- attention_out: bfloat16 [4, 1024, 2048], P('grp', 'seq')
- grad_query: bfloat16 [4, 1024, 2048], P('grp', 'seq')
- grad_key: bfloat16 [4, 1024, 2048], P('grp', 'seq')
- grad_value: bfloat16 [4, 1024, 2048], P('grp', 'seq')
- expert_grad: bfloat16 [16, 704, 2048], P('seq', 'grp')
Inputs may be any that keep to these rules, and one draw needn't show every extreme that they name: `routes`: the 6 experts of a token differ. Among the 128 tokens of one device (aligned blocks of the positions of a sequence) no expert is named more than 128 times, and in every sequence some expert is named exactly 128 times by the tokens of each device. Expert ids are small integers and may be packed several to a word whenever they are sent.
All inputs are finite; a program needn't handle non-finite values.
Results may differ from a plain program's by a relative error of at most 0.04.
Values may be sent and summed in bfloat16 or wider, within the bound.
A program may use at most 192 MiB of HBM per device.

v0:
```python
import jax
import jax.numpy as jnp
from jax import lax
from jax.sharding import PartitionSpec as P

HEADS = 16
TOPK = 6
EXP_DEV = 2


PRECISE = lax.Precision.HIGHEST


def carried_in(array, axis, join, neutral, backward):
    count = lax.axis_size(axis)
    place = lax.axis_index(axis)
    ahead = count - 1 - place if backward else place
    gathered = lax.all_gather(array.astype(jnp.bfloat16), axis)
    state = jnp.zeros_like(array) + jnp.asarray(neutral, array.dtype)

    def one(lap, state):
        source = count - 1 - lap if backward else lap
        return join(state, lax.dynamic_index_in_dim(gathered, source, 0, False).astype(array.dtype))

    return lax.fori_loop(0, ahead, one, state)


def add_states(first_term, second_term):
    return first_term + second_term


def per_device(query, key_in, value, cotangent, routes, gates, hidden):
    tokens = query.shape[1]
    width = query.shape[2]
    head_dim = width // HEADS
    hidden_units = hidden.shape[3]
    seq_count = lax.axis_size("seq")
    seq_index = lax.axis_index("seq")
    query_raw = query[0].reshape(tokens, HEADS, head_dim)
    key_raw = key_in[0].reshape(tokens, HEADS, head_dim)
    value_raw = value[0].reshape(tokens, HEADS, head_dim)
    grad_raw = cotangent[0].reshape(tokens, HEADS, head_dim)
    query_full = query_raw.astype(jnp.float32)
    key_full = key_raw.astype(jnp.float32)
    value_full = value_raw.astype(jnp.float32)
    grad_out = grad_raw.astype(jnp.float32)
    position = seq_index * tokens + jnp.arange(tokens, dtype=jnp.int32)
    scaling = 1.0 / jnp.sqrt(head_dim * (position + 1).astype(jnp.float32))
    row_scale = scaling[:, None, None]
    causal = jnp.tril(jnp.ones((tokens, tokens), jnp.float32))
    state_sum = jnp.einsum("thd,the->hde", key_raw, value_raw, preferred_element_type=jnp.float32)
    grad_sum = jnp.einsum("thd,the->hde", query_full * row_scale, grad_out, precision=PRECISE)
    empty = jnp.zeros_like(state_sum)
    prefix_state = carried_in(state_sum, "seq", add_states, empty, False)
    after_state = carried_in(grad_sum, "seq", add_states, empty, True)
    scores = (
        jnp.einsum("thd,uhd->htu", query_raw, key_raw, preferred_element_type=jnp.float32) * causal
    )
    outputs = jnp.einsum("htu,uhe->the", scores, value_full, precision=PRECISE)
    outputs = (
        outputs + jnp.einsum("thd,hde->the", query_full, prefix_state, precision=PRECISE)
    ) * row_scale
    grad_scores = (
        jnp.einsum("the,uhe->htu", grad_raw, value_raw, preferred_element_type=jnp.float32) * causal
    )
    grad_q = jnp.einsum("htu,uhd->thd", grad_scores, key_full, precision=PRECISE)
    grad_q = (
        grad_q + jnp.einsum("the,hde->thd", grad_out, prefix_state, precision=PRECISE)
    ) * row_scale
    col_scale = scaling[None, :, None]
    weighted = scores * col_scale
    grad_weighted = grad_scores * col_scale
    grad_k = jnp.einsum("htu,thd->uhd", grad_weighted, query_full, precision=PRECISE)
    grad_k = grad_k + jnp.einsum("uhe,hde->uhd", value_full, after_state, precision=PRECISE)
    grad_v = jnp.einsum("htu,the->uhe", weighted, grad_out, precision=PRECISE)
    grad_v = grad_v + jnp.einsum("uhd,hde->uhe", key_full, after_state, precision=PRECISE)

    def to_shard(array):
        return array.reshape(1, tokens, width).astype(jnp.bfloat16)

    experts_total = EXP_DEV * seq_count
    capacity = tokens * TOPK * 8 // (experts_total * 3)
    assigned = tokens * TOPK
    flat_ids = routes[0].reshape(assigned)
    expert_range = jnp.arange(experts_total, dtype=jnp.int32)
    matches = (flat_ids[:, None] == expert_range[None, :]).astype(jnp.int32)
    ranking = jnp.sum((jnp.cumsum(matches, axis=0) - matches) * matches, axis=1)
    slot_index = flat_ids * capacity + ranking
    scaled = (
        gates[0].reshape(assigned, 1)
        * hidden[0].reshape(assigned, hidden_units).astype(jnp.float32)
    ).astype(jnp.bfloat16)
    hidden_slots = (
        jnp.zeros((experts_total * capacity, hidden_units), jnp.bfloat16).at[slot_index].set(scaled)
    )
    hidden_slots = hidden_slots.reshape(seq_count, EXP_DEV, capacity, hidden_units)
    token_index = jnp.arange(assigned, dtype=jnp.int32) // TOPK
    all_routes = lax.all_gather(routes, "seq", axis=1, tiled=True)[0].reshape(seq_count, assigned)
    arrived_hidden = lax.all_to_all(hidden_slots, "seq", split_axis=0, concat_axis=0, tiled=True)
    all_cotangent = lax.all_gather(cotangent, "seq", axis=1, tiled=True)[0]
    own_experts = seq_index * EXP_DEV + jnp.arange(EXP_DEV, dtype=jnp.int32)
    source_match = (all_routes[:, None, :] == own_experts[None, :, None]).astype(jnp.int32)
    source_rank = jnp.cumsum(source_match, axis=2) - source_match
    slot_range = jnp.arange(capacity, dtype=jnp.int32)
    placed = (source_match[..., None] == 1) & (source_rank[..., None] == slot_range)
    token_of_slot = jnp.sum(jnp.where(placed, token_index[None, None, :, None], 0), axis=2)
    wanted = (
        jnp.arange(seq_count, dtype=jnp.int32)[:, None, None] * tokens + token_of_slot
    ).reshape(-1)
    cot_rows = jnp.take(all_cotangent, wanted, axis=0).reshape(seq_count, EXP_DEV, capacity, width)
    group_term = jnp.einsum(
        "sxcf,sxcd->xfd", arrived_hidden, cot_rows, preferred_element_type=jnp.float32
    )
    rounded = lax.optimization_barrier(group_term.astype(jnp.bfloat16)).astype(jnp.float32)
    expert_grad = lax.psum_scatter(
        rounded.astype(jnp.bfloat16), "grp", scatter_dimension=1, tiled=True
    )
    return (to_shard(outputs), to_shard(grad_q), to_shard(grad_k), to_shard(grad_v), expert_grad)


def solution(mesh):
    in_specs = (
        P("grp", "seq", None),
        P("grp", "seq", None),
        P("grp", "seq", None),
        P("grp", "seq", None),
        P("grp", "seq", None),
        P("grp", "seq", None),
        P("grp", "seq", None, None),
    )
    out_specs = (
        P("grp", "seq", None),
        P("grp", "seq", None),
        P("grp", "seq", None),
        P("grp", "seq", None),
        P("seq", "grp", None),
    )
    return jax.shard_map(
        per_device, mesh=mesh, in_specs=in_specs, out_specs=out_specs, check_vma=False
    )
```

profile of v0, /device:TPU:0, one launch (start us, length us, event | category | flops | bytes accessed | tf_op | source)
XLA Modules:
  0.0 343.7 jit_solution(8610637813266482346)
XLA Ops:
  10.6 2.0 convolution_convert_fusion.1
  17.2 3.1 copy.167
  20.4 4.0 %reshape.242 = f32[768,704]{1,0:T(8,128)} reshape(f32[1,128,6,704]{3,2,1,0:T(8,128)} %copy.167) | data formatting | bytes 4325376 | tf_op jit(solution)/shard_map/convert_element_type | solution.py:91
  24.7 11.6 %scatter_custom_fusion = bf16[2048,704]{1,0:T(8,128)(2,1)} fusion(s32[768]{0:T(1024)S(1)} %fusion.41, bf16[]{:T(256)} %constant.88.clone.1, f32[768,704]{1,0:T(8,128)} %reshape.242, f32[768]{0:T(1024)S(1)} %mul.124), kind=kCustom, calls=%fused_computation.13 | custom fusion | flops 1081344 | bytes 5050370 | tf_op jit(solution)/shard_map/scatter | solution.py:94
  36.4 4.7 %copy.169 = bf16[8,2,128,704]{2,3,1,0:T(8,128)(2,1)} copy(bf16[8,2,128,704]{3,2,1,0:T(8,128)(2,1)} %bitcast.122) | data formatting | bytes 5767168 | tf_op jit(solution)/shard_map/reshape | solution.py:96
  41.1 7.2 %all-to-all-start = ((bf16[8,2,128,704]{2,3,1,0:T(8,128)(2,1)}), bf16[8,2,128,704]{2,3,1,0:T(8,128)(2,1)}, u32[]{:S(2)}, u32[]{:S(2)}) async-start(bf16[8,2,128,704]{2,3,1,0:T(8,128)(2,1)} %copy.169), calls=%async_computation | async-start | bytes 5767168 | tf_op jit(solution)/shard_map/all_to_all | solution.py:99
  48.3 93.2 %all_gather.22 = s32[1,1024,6]{1,0,2:T(1,128)S(1)} all-gather(s32[1,128,6]{1,0,2:T(1,128)S(1)} %copy-done.2), channel_id=1, replica_groups=mesh['seq'=8,'grp'=4] {'seq'}, dimensions={1}, use_global_device_ids=true | all-gather | bytes 27648 | tf_op jit(solution)/shard_map/all_gather | solution.py:98
  142.4 3.4 reduce-window.16
  146.5 4.9 %select_reduce_fusion = s32[8,2,128]{2,1,0:T(2,128)S(1)} fusion(s32[768]{0:T(1024)S(1)} %add_select_fusion, s32[8,2,768]{2,1,0:T(2,128)S(1)} %copy.175, pred[8,2,768]{2,1,0:T(4,128)(4,1)S(1)} %copy.171), kind=kLoop, calls=%fused_computation.8 | loop fusion | flops 6289408 | bytes 72704 | tf_op jit(solution)/shard_map/reduce_sum | solution.py:106
  151.6 19.1 %gather_fusion = bf16[2048,2048]{1,0:T(8,128)(2,1)} fusion(bf16[1024,2048]{1,0:T(8,128)(2,1)} %bitcast.109, s32[2048]{0:T(1024)S(1)} %broadcast_clamp_fusion), kind=kCustom, calls=%fused_computation | custom fusion | bytes 16785408 | tf_op jit(solution)/shard_map/jit(_take)/gather | solution.py:110
  170.7 11.2 %bitcast_convert_fusion = bf16[2,704,2048]{2,1,0:T(8,128)(2,1)} fusion(bf16[8,2,128,704]{2,3,1,0:T(8,128)(2,1)} %all-to-all-done, bf16[8,2,128,2048]{3,2,1,0:T(8,128)(2,1)} %bitcast.123, pred[8,2,128]{2,1,0:T(4,128)(4,1)S(1)} %get-tuple-element.127), kind=kOutput, calls=%fused_computation.4 | convolution fusion | flops 5912657920 | bytes 17041408 | tf_op jit(solution)/shard_map/sxcf,sxcd->xfd/dot_general | solution.py:111
  182.9 2.2 convolution_bitcast_fusion.5
  185.2 2.2 convolution_bitcast_fusion.7
  187.4 1.7 convolution_bitcast_fusion.3
  189.1 1.7 convolution_bitcast_fusion.1
  190.8 15.8 %all-gather.10.cloned.1.call-done = bf16[128,128,128]{2,1,0:T(8,128)(2,1)} async-done(((bf16[16,128,128]{2,1,0:T(8,128)(2,1)}), bf16[128,128,128]{2,1,0:T(8,128)(2,1)}) %all-gather.10.cloned.1.call-update) | async-done | bytes 4194320 | tf_op jit(solution)/shard_map/all_gather | solution.py:18
  206.7 9.2 %while.23 = (s32[]{:T(128)}, f32[16,128,128]{2,1,0:T(8,128)S(1)}, s32[]{:T(128)}, bf16[8,16,128,128]{3,2,1,0:T(8,128)(2,1)}, s32[]{:T(128)}, /*index=5*/s32[]{:T(128)}, s32[]{:T(128)}, s32[]{:T(128)}) while((s32[]{:T(128)}, f32[16,128,128]{2,1,0:T(8,128)S(1)}, s32[]{:T(128)}, bf16[8,16,128,128]{3,2,1,0:T(8,128)(2,1)}, s32[]{:T(128)}, ...), condition=%wide.region_3.4_spmd, body=%wide.region_2.3_spmd.sunk | while | flops 524294 | bytes 2621575 | solution.py:25
  216.0 3.3 fusion.15
  219.3 2.0 copy.178
  221.4 2.2 fusion.16
  224.6 56.5 %all-gather.8.cloned.1.call-done = bf16[128,128,128]{2,1,0:T(8,128)(2,1)} async-done(((bf16[16,128,128]{2,1,0:T(8,128)(2,1)}), bf16[128,128,128]{2,1,0:T(8,128)(2,1)}) %all-gather.8.cloned.1.call-update) | async-done | bytes 4194320 | tf_op jit(solution)/shard_map/all_gather | solution.py:18
  281.4 1.9 fusion.18
  284.3 2.2 fusion.17
  287.5 49.6 %reduce-scatter.2.cloned.1.call-done = bf16[2,176,2048]{2,1,0:T(8,128)(2,1)} async-done(((bf16[2,704,2048]{2,1,0:T(8,128)(2,1)}), bf16[2,176,2048]{2,1,0:T(8,128)(2,1)}) %reduce-scatter.2.cloned.1.call-update) | async-done | bytes 1441808 | tf_op jit(solution)/shard_map/reduce_scatter | solution.py:115
  (73 shorter events, 23.5 us)
Async XLA Ops:
  7.2 5.5 %copy-start = (bf16[1,128,2048]{2,1,0:T(8,128)(2,1)S(1)}, bf16[1,128,2048]{2,1,0:T(8,128)(2,1)}, u32[]{:S(2)}) copy-start(bf16[1,128,2048]{2,1,0:T(8,128)(2,1)} %param.13) | copy-start | bytes 1572868
  7.2 5.7 %copy-start.1 = (bf16[1,128,2048]{2,1,0:T(8,128)(2,1)S(1)}, bf16[1,128,2048]{2,1,0:T(8,128)(2,1)}, u32[]{:S(2)}) copy-start(bf16[1,128,2048]{2,1,0:T(8,128)(2,1)} %param.12) | copy-start | bytes 1572868
  7.2 144.4 %all-gather.6.cloned.1.call-start = ((), (), s32[]{:S(2)}) async-start(), calls=%async_computation.2 | async-start | bytes 4718592 | tf_op jit(solution)/shard_map/all_gather | solution.py:100
  7.9 198.7 %all-gather.10.cloned.1.call-start = ((), (), s32[]{:S(2)}) async-start(), calls=%async_computation.5 | async-start | bytes 4718592 | tf_op jit(solution)/shard_map/all_gather | solution.py:18
  12.6 1.9 copy-start.2
  12.7 268.4 %all-gather.8.cloned.1.call-start = ((), (), s32[]{:S(2)}) async-start(), calls=%async_computation.4 | async-start | bytes 4718592 | tf_op jit(solution)/shard_map/all_gather | solution.py:18
  20.4 4.0 %copy-start.3 = (f32[1,128,6]{1,0,2:T(1,128)S(1)}, f32[1,128,6]{1,0,2:T(1,128)}, u32[]{:S(2)}) copy-start(f32[1,128,6]{1,0,2:T(1,128)} %param.16) | copy-start | bytes 9220
  41.1 129.6 %all-to-all-start = ((bf16[8,2,128,704]{2,3,1,0:T(8,128)(2,1)}), bf16[8,2,128,704]{2,3,1,0:T(8,128)(2,1)}, u32[]{:S(2)}, u32[]{:S(2)}) async-start(bf16[8,2,128,704]{2,3,1,0:T(8,128)(2,1)} %copy.169), calls=%async_computation | async-start | bytes 5767168 | tf_op jit(solution)/shard_map/all_to_all | solution.py:99
  48.3 288.9 %reduce-scatter.2.cloned.1.call-start = ((), (), s32[]{:S(2)}) async-start(), calls=%async_computation.3 | async-start | bytes 7208960 | tf_op jit(solution)/shard_map/reduce_scatter | solution.py:115
Sparse Core Ops, SparseCore 0:
  10.1 105.8 all-gather.5
  118.7 87.8 all-gather.9
  209.4 71.6 all-gather.7
  284.0 53.1 reduce-scatter.1
where the time goes:
time: 345 us; the launch traced here: 344 us
  waiting for transfers between devices  123 us (36%)
  blocking collectives  93.2 us (27%)
  local copies, waits for them, and re-layouts  41.9 us (12%)
  matrix products  32.9 us (10%)
  other arithmetic  31.2 us (9%)
  between operations  14.1 us (4%)
  starting transfers between devices  7.37 us (2%)
    all_gather x1, blocking collectives, per_device(): lax.all_gather(routes, 'seq', axis=1, tiled=True)[0]  93.2 us
    all_gather x2, waiting for transfers between devices, carried_in(): gathered = lax.all_gather(array.astype(jnp.bfloat16), axis)  72.3 us
    reduce_scatter x1, waiting for transfers between devices, per_device(): lax.psum_scatter(rounded.astype(jnp.bfloat16), 'grp', scatter_dimension=1...  49.6 us
    gather x1, local copies, waits for them, and re-layouts, per_device(): jnp.take(all_cotangent, wanted, axis=0)  19.1 us
    scatter x1, other arithmetic, per_device(): jnp.zeros((experts_total * capacity, hidden_units), jnp.bfloat16)  11.6 us
    dot_general x1, matrix products, per_device(): jnp.einsum('sxcf,sxcd->xfd', arrived_hidden, cot_rows, preferred_element_...  11.2 us
    add x7, other arithmetic, add_states(): return first_term + second_term  9.02 us
    all_to_all x1, starting transfers between devices, per_device(): lax.all_to_all(hidden_slots, 'seq', split_axis=0, concat_axis=0, tiled=True)  7.21 us
  transfers between devices with their start and end apart: 5, of which 3 were waited for; matrix products, arithmetic and copies ran while one was open for 31% of the time, Pallas kernels for 0%

commit v1 on v0

v1 whole, which is shorter than its diff:
```python
import functools

import jax
import jax.numpy as jnp
from jax import lax
from jax.experimental import pallas as pl
from jax.experimental.pallas import tpu as pltpu
from jax.sharding import PartitionSpec as P

HEADS = 16
EXP_DEV = 2
BF = jnp.bfloat16
F32 = jnp.float32
VMEM_BYTES = 56 * 1024 * 1024


def dot(a, b, ca, cb):
    return lax.dot_general(a, b, (((ca,), (cb,)), ((), ())), preferred_element_type=F32)


def exchange_kernel(
    inner,
    q_ref, k_ref, v_ref, g_ref, hid_ref, routes_ref,
    out_ref, gq_ref, gk_ref, gv_ref, cotg_ref, arr_ref,
    slots, own_state, peer_state, total_state, chain_in, chain_out, carried, score_ref, gscore_ref,
    cot_send, cot_recv, slot_send, slot_recv, st_send, st_recv, ch_send, ch_recv, local_sem,
):
    count = lax.axis_size("seq")
    outer = count // inner
    me = lax.axis_index("seq")
    row = me // inner
    col = me % inner
    tokens = q_ref.shape[0]
    topk = hid_ref.shape[0]
    head = q_ref.shape[1] // HEADS

    def remote(src, dst, send, recv, target):
        return pltpu.make_async_remote_copy(
            src_ref=src, dst_ref=dst, send_sem=send, recv_sem=recv,
            device_id={"seq": target}, device_id_type=pl.DeviceIdType.MESH,
        )

    barrier = pltpu.get_barrier_semaphore()

    def greet(step, carry):
        pl.semaphore_signal(
            barrier, inc=1, device_id={"seq": lax.rem(me + step, count)},
            device_id_type=pl.DeviceIdType.MESH,
        )
        return carry

    lax.fori_loop(1, count, greet, 0)
    pl.semaphore_wait(barrier, count - 1)

    def cot_copy(origin, src, lane, target):
        return remote(src, cotg_ref.at[origin], cot_send.at[origin, lane], cot_recv.at[origin], target)

    def cot_spread(origin, src, up, down, act):
        if up is not None:
            @pl.when(up)
            def _():
                act(cot_copy(origin, src, 0, me + inner))
        if down is not None:
            @pl.when(down)
            def _():
                act(cot_copy(origin, src, 1, me - inner))
        for off in range(1, inner):
            act(cot_copy(origin, src, 1 + off, row * inner + lax.rem(col + off, inner)))

    def cot_forward(step, act, wait):
        @pl.when(row >= step)
        def _():
            origin = me - step * inner
            if wait:
                cot_copy(origin, cotg_ref.at[origin], 0, origin).wait_recv()
            cot_spread(origin, cotg_ref.at[origin], row + 1 < outer, None, act)

        @pl.when(row + step < outer)
        def _():
            origin = me + step * inner
            if wait:
                cot_copy(origin, cotg_ref.at[origin], 0, origin).wait_recv()
            cot_spread(origin, cotg_ref.at[origin], None, row >= 1, act)

    start = lambda copy: copy.start()
    finish = lambda copy: copy.wait_send()

    cot_spread(me, g_ref, row + 1 < outer, row >= 1, start)
    own_cot = pltpu.make_async_copy(g_ref, cotg_ref.at[me], local_sem.at[0])
    own_cot.start()

    position = me * tokens + lax.broadcasted_iota(jnp.int32, (tokens, 1), 0)
    scaling = lax.rsqrt((head * (position + 1)).astype(F32))
    causal = lax.broadcasted_iota(jnp.int32, (tokens, tokens), 0) >= lax.broadcasted_iota(
        jnp.int32, (tokens, tokens), 1
    )

    def heads_of(h):
        return pl.ds(pl.multiple_of(h * head, head), head)

    def states(h, carry):
        at = heads_of(h)
        q, k, v, g = q_ref[:, at], k_ref[:, at], v_ref[:, at], g_ref[:, at]
        own_state[0, at, :] = dot(k, v, 0, 0).astype(BF)
        own_state[1, at, :] = dot((q.astype(F32) * scaling).astype(BF), g, 0, 0).astype(BF)
        return carry

    lax.fori_loop(0, HEADS, states, 0)

    def state_copy(off):
        return remote(
            own_state, peer_state.at[col], st_send.at[off], st_recv.at[col],
            row * inner + lax.rem(col + off, inner),
        )

    for off in range(1, inner):
        state_copy(off).start()

    def fill(target):
        for x in range(EXP_DEV):
            expert = target * EXP_DEV + x
            total = jnp.zeros((tokens, hid_ref.shape[2]), F32)
            for j in range(topk):
                chosen = routes_ref[:, j : j + 1] == expert
                total = total + jnp.where(chosen, hid_ref[j].astype(F32), 0.0)
            slots[target, x] = total.astype(BF)

    def slot_copy(off):
        target = lax.rem(me + off, count)
        return remote(
            slots.at[target], arr_ref.at[:, pl.ds(pl.multiple_of(me * tokens, tokens), tokens), :],
            slot_send.at[off], slot_recv.at[me], target,
        )

    def send_slots(off, carry):
        fill(lax.rem(me + off, count))
        slot_copy(off).start()
        return carry

    lax.fori_loop(1, count, send_slots, 0)
    fill(me)
    own_slots = pltpu.make_async_copy(
        slots.at[me], arr_ref.at[:, pl.ds(pl.multiple_of(me * tokens, tokens), tokens), :],
        local_sem.at[1],
    )
    own_slots.start()

    def state_wait(off):
        source = lax.rem(col + off, inner)
        remote(
            own_state, peer_state.at[source], st_send.at[off], st_recv.at[source],
            row * inner + source,
        ).wait_recv()

    for off in range(1, inner):
        state_wait(off)
    peer_state[col] = own_state[...]

    def sum_rows(h, carry):
        at = heads_of(h)
        for which in range(2):
            total = jnp.zeros((head, head), F32)
            part = jnp.zeros((head, head), F32)
            for c in range(inner):
                block = peer_state[c, which, at, :].astype(F32)
                total = total + block
                counts = (c < col) if which == 0 else (c > col)
                part = part + jnp.where(counts, block, 0.0)
            total_state[which, at, :] = total
            carried[which, at, :] = part
        return carry

    lax.fori_loop(0, HEADS, sum_rows, 0)

    def chain_copy(which):
        target = me + inner if which == 0 else me - inner
        return remote(
            chain_out.at[which], chain_in.at[which], ch_send.at[which], ch_recv.at[which], target
        )

    def chain_step(which, first, last):
        if not first:
            chain_copy(which).wait_recv()

        def one(h, carry):
            at = heads_of(h)
            here = total_state[which, at, :]
            if not first:
                before = chain_in[which, at, :].astype(F32)
                carried[which, at, :] = carried[which, at, :] + before
                here = here + before
            if not last:
                chain_out[which, at, :] = here.astype(BF)
            return carry

        lax.fori_loop(0, HEADS, one, 0)
        if not last:
            chain_copy(which).start()

    def local_scores(h, carry):
        at = heads_of(h)
        q, k, v, g = q_ref[:, at], k_ref[:, at], v_ref[:, at], g_ref[:, at]
        score_ref[h] = jnp.where(causal, dot(q, k, 1, 1), 0.0).astype(BF)
        gscore_ref[h] = jnp.where(causal, dot(g, v, 1, 1), 0.0).astype(BF)
        return carry

    for step in range(outer):
        @pl.when(row == step)
        def _():
            chain_step(0, step == 0, step == outer - 1)

        @pl.when(row == outer - 1 - step)
        def _():
            chain_step(1, step == 0, step == outer - 1)

        if step == 0:
            lax.fori_loop(0, HEADS, local_scores, 0)
        if step >= 1:
            cot_forward(step, start, True)

    def finals(h, carry):
        at = heads_of(h)
        q, k, v, g = q_ref[:, at], k_ref[:, at], v_ref[:, at], g_ref[:, at]
        before = carried[0, at, :].astype(BF)
        after = carried[1, at, :].astype(BF)
        scores = score_ref[h]
        gscores = gscore_ref[h]
        weighted = (scores.astype(F32) * scaling).astype(BF)
        gweighted = (gscores.astype(F32) * scaling).astype(BF)
        out_ref[:, at] = ((dot(scores, v, 1, 0) + dot(q, before, 1, 0)) * scaling).astype(BF)
        gq_ref[:, at] = ((dot(gscores, k, 1, 0) + dot(g, before, 1, 1)) * scaling).astype(BF)
        gk_ref[:, at] = (dot(gweighted, q, 0, 0) + dot(v, after, 1, 1)).astype(BF)
        gv_ref[:, at] = (dot(weighted, g, 0, 0) + dot(k, after, 1, 0)).astype(BF)
        return carry

    lax.fori_loop(0, HEADS, finals, 0)

    def cot_last(off, carry):
        source = lax.rem(col + off, inner)

        def one(line, carry):
            origin = line * inner + source
            cot_copy(origin, cotg_ref.at[origin], 0, row * inner + source).wait_recv()
            return carry

        return lax.fori_loop(0, outer, one, carry)

    lax.fori_loop(1, inner, cot_last, 0)

    def slots_last(off, carry):
        source = lax.rem(me + off, count)
        remote(
            slots.at[source],
            arr_ref.at[:, pl.ds(pl.multiple_of(source * tokens, tokens), tokens), :],
            slot_send.at[off], slot_recv.at[source], source,
        ).wait_recv()
        slot_copy(off).wait_send()
        return carry

    lax.fori_loop(1, count, slots_last, 0)
    own_cot.wait()
    own_slots.wait()
    cot_spread(me, g_ref, row + 1 < outer, row >= 1, finish)
    for step in range(1, outer):
        cot_forward(step, finish, False)
    for off in range(1, inner):
        state_copy(off).wait_send()

    @pl.when(row < outer - 1)
    def _():
        chain_copy(0).wait_send()

    @pl.when(row >= 1)
    def _():
        chain_copy(1).wait_send()


def exchange(query, key_in, value, cotangent, hidden, routes):
    count = lax.axis_size("seq")
    inner = 2 if count <= 8 else 8
    tokens, width = query.shape
    head = width // HEADS
    units = hidden.shape[2]
    vmem = pl.BlockSpec(memory_space=pltpu.VMEM)
    anywhere = pl.BlockSpec(memory_space=pl.ANY)
    flat = jax.ShapeDtypeStruct((tokens, width), BF)
    dma = pltpu.SemaphoreType.DMA
    return pl.pallas_call(
        functools.partial(exchange_kernel, inner),
        out_shape=(
            flat, flat, flat, flat,
            jax.ShapeDtypeStruct((count, tokens, width), BF),
            jax.ShapeDtypeStruct((EXP_DEV, count * tokens, units), BF),
        ),
        in_specs=[vmem] * 6,
        out_specs=(vmem, vmem, vmem, vmem, anywhere, anywhere),
        scratch_shapes=[
            pltpu.VMEM((count, EXP_DEV, tokens, units), BF),
            pltpu.VMEM((2, width, head), BF),
            pltpu.VMEM((inner, 2, width, head), BF),
            pltpu.VMEM((2, width, head), F32),
            pltpu.VMEM((2, width, head), BF),
            pltpu.VMEM((2, width, head), BF),
            pltpu.VMEM((2, width, head), F32),
            pltpu.VMEM((HEADS, tokens, tokens), BF),
            pltpu.VMEM((HEADS, tokens, tokens), BF),
            dma((count, inner + 1)), dma((count,)),
            dma((count,)), dma((count,)),
            dma((inner,)), dma((inner,)),
            dma((2,)), dma((2,)),
            dma((2,)),
        ],
        compiler_params=pltpu.CompilerParams(
            collective_id=0, has_side_effects=True, vmem_limit_bytes=VMEM_BYTES
        ),
        name="exchange",
    )(query, key_in, value, cotangent, hidden, routes)


def per_device(query, key_in, value, cotangent, routes, gates, hidden):
    scaled = (gates[0][:, :, None] * hidden[0].astype(F32)).astype(BF).transpose(1, 0, 2)
    outputs, grad_q, grad_k, grad_v, all_cot, arrived = exchange(
        query[0], key_in[0], value[0], cotangent[0], scaled, routes[0]
    )
    all_cot = all_cot.reshape(-1, all_cot.shape[2])
    group_term = jnp.einsum("xtf,td->xfd", arrived, all_cot, preferred_element_type=F32)
    expert_grad = lax.psum_scatter(
        group_term.astype(BF), "grp", scatter_dimension=1, tiled=True
    )
    return (outputs[None], grad_q[None], grad_k[None], grad_v[None], expert_grad)


def solution(mesh):
    rows = P("grp", "seq", None)
    in_specs = (rows, rows, rows, rows, rows, rows, P("grp", "seq", None, None))
    out_specs = (rows, rows, rows, rows, P("seq", "grp", None))
    return jax.shard_map(
        per_device, mesh=mesh, in_specs=in_specs, out_specs=out_specs, check_vma=False
    )
```

time: 345 us -> 224 us (0.65)
  Pallas kernels: 0 us -> 135 us
  blocking collectives: 93.2 us -> 0 us
  waiting for transfers between devices: 123 us -> 55.1 us
  local copies, waits for them, and re-layouts: 41.9 us -> 6.84 us
  other arithmetic: 31.2 us -> 1.27 us
  matrix products: 32.9 us -> 10.7 us
  starting transfers between devices: 7.37 us -> 0.04 us
    pallas_call x0 -> x1, Pallas kernels: none -> 135 us  [exchange(): pl.pallas_call(functools.partial(exchange_kernel, inner), out_shape=(flat...]
    all_gather x1 -> x0, blocking collectives: 93.2 us -> none  [per_device(): lax.all_gather(routes, 'seq', axis=1, tiled=True)[0]]
    all_gather x3 -> x0, waiting for transfers between devices: 72.3 us -> none  [the longest x2 72.3 us: carried_in(): gathered = lax.all_gather(array.astype(jnp.bfloat16), axis)]
    dot_general x13 -> x1, matrix products: 32.9 us -> 10.7 us  [per_device(): jnp.einsum('xtf,td->xfd', arrived, all_cot, preferred_element_type=F32)]
    gather x1 -> x0, local copies, waits for them, and re-layouts: 19.1 us -> none  [per_device(): jnp.take(all_cotangent, wanted, axis=0)]
    scatter x1 -> x0, other arithmetic: 11.6 us -> none  [per_device(): jnp.zeros((experts_total * capacity, hidden_units), jnp.bfloat16)]
    add x8 -> x0, other arithmetic: 9.02 us -> none  [the longest x7 9.02 us: add_states(): return first_term + second_term]
    all_to_all x1 -> x0, starting transfers between devices: 7.21 us -> none  [per_device(): lax.all_to_all(hidden_slots, 'seq', split_axis=0, concat_axis=0, tiled=True)]
  transfers between devices with their start and end apart: 5 -> 1, of which waited for: 3 -> 1; matrix products, arithmetic and copies ran while one was open for 31% -> 0% of each run, Pallas kernels for 0% -> 0%
where the time goes in v1:
time: 224 us; the launch traced here: 223 us
  Pallas kernels  135 us (60%)
  waiting for transfers between devices  55.1 us (25%)
  between operations  14.1 us (6%)
  matrix products  10.7 us (5%)
  local copies, waits for them, and re-layouts  6.84 us (3%)
    pallas_call x1, Pallas kernels, exchange(): pl.pallas_call(functools.partial(exchange_kernel, inner), out_shape=(flat...  135 us
    reduce_scatter x1, waiting for transfers between devices, per_device(): lax.psum_scatter(group_term.astype(BF), 'grp', scatter_dimension=1, tiled...  55.1 us
    dot_general x1, matrix products, per_device(): jnp.einsum('xtf,td->xfd', arrived, all_cot, preferred_element_type=F32)  10.7 us
    unnamed x15, local copies, waits for them, and re-layouts  6.84 us
  transfers between devices with their start and end apart: 1, of which 1 were waited for; matrix products, arithmetic and copies ran while one was open for 0% of the time, Pallas kernels for 0%

profile of v1, /device:TPU:0, one launch (start us, length us, event | category | flops | bytes accessed | tf_op | source)
XLA Modules:
  0.0 223.3 jit_solution(15069241518961785309)
XLA Ops:
  7.2 0.0 reduce-scatter.2.cloned.1.call-start
  7.2 0.7 copy.18
  7.9 1.4 copy.13
  9.3 1.5 copy.12
  10.9 1.3 fusion.1.hid_ref
  12.1 135.2 %exchange.1 = (bf16[128,2048]{1,0:T(8,128)(2,1)}, bf16[128,2048]{1,0:T(8,128)(2,1)}, bf16[128,2048]{1,0:T(8,128)(2,1)}, bf16[128,2048]{1,0:T(8,128)(2,1)}, bf16[...) custom-call(bf16[128,2048]{1,0:T(8,128)(2,1)} %bitcast.22, bf16[128,2048]{1,0:T(8,128)(2,1)} %bitcast.23, ...), custom_call_target="tpu_custom_call" | custom-call | tf_op jit(solution)/shard_map/exchange/pallas_call | solution.py:288
  147.3 10.7 %convolution_convert_fusion = bf16[2,704,2048]{2,1,0:T(8,128)(2,1)} fusion(bf16[2,1024,704]{2,1,0:T(8,128)(2,1)} %get-tuple-element.15, bf16[1024,2048,1]{1,0,2:T(8,128)(2,1)} %bitcast.32), kind=kOutput, calls=%fused_computation | convolution fusion | flops 5908463616 | bytes 12845056 | tf_op jit(solution)/shard_map/xtf,td->xfd/dot_general | solution.py:326
  158.1 0.0 copy-start.3
  158.1 0.0 copy-start.2
  158.1 0.0 copy-start.1
  158.1 0.0 copy-start
  158.1 0.0 reduce-scatter.2.cloned.1.call-update
  158.1 55.1 %reduce-scatter.2.cloned.1.call-done = bf16[2,176,2048]{2,1,0:T(8,128)(2,1)} async-done(((bf16[2,704,2048]{2,1,0:T(8,128)(2,1)}), bf16[2,176,2048]{2,1,0:T(8,128)(2,1)}) %reduce-scatter.2.cloned.1.call-update) | async-done | bytes 1441808 | tf_op jit(solution)/shard_map/reduce_scatter | solution.py:327
  213.2 0.0 copy-done.3
  213.2 0.8 copy.23
  214.0 0.0 copy-done.2
  214.0 0.8 copy.24
  214.8 0.0 copy-done.1
  214.8 0.8 copy.25
  215.6 0.0 copy-done
  215.6 0.8 copy.26
Async XLA Ops:
  7.2 206.1 %reduce-scatter.2.cloned.1.call-start = ((), (), s32[]{:S(2)}) async-start(), calls=%async_computation.1 | async-start | bytes 7208960 | tf_op jit(solution)/shard_map/reduce_scatter | solution.py:327
  158.1 55.2 %copy-start.3 = (bf16[128,2048]{1,0:T(8,128)(2,1)S(1)}, bf16[128,2048]{1,0:T(8,128)(2,1)}, u32[]{:S(2)}) copy-start(bf16[128,2048]{1,0:T(8,128)(2,1)} %get-tuple-element.11) | copy-start | bytes 1572868
  158.1 56.0 %copy-start.2 = (bf16[128,2048]{1,0:T(8,128)(2,1)S(1)}, bf16[128,2048]{1,0:T(8,128)(2,1)}, u32[]{:S(2)}) copy-start(bf16[128,2048]{1,0:T(8,128)(2,1)} %get-tuple-element.12) | copy-start | bytes 1572868
  158.1 56.8 %copy-start.1 = (bf16[128,2048]{1,0:T(8,128)(2,1)S(1)}, bf16[128,2048]{1,0:T(8,128)(2,1)}, u32[]{:S(2)}) copy-start(bf16[128,2048]{1,0:T(8,128)(2,1)} %get-tuple-element.13) | copy-start | bytes 1572868
  158.1 57.5 %copy-start = (bf16[128,2048]{1,0:T(8,128)(2,1)S(1)}, bf16[128,2048]{1,0:T(8,128)(2,1)}, u32[]{:S(2)}) copy-start(bf16[128,2048]{1,0:T(8,128)(2,1)} %get-tuple-element.14) | copy-start | bytes 1572868
Sparse Core Ops, SparseCore 0:
  158.2 54.9 reduce-scatter.1

commit v2 on v1

v2 whole, which is shorter than its diff:
```python
import functools

import jax
import jax.numpy as jnp
from jax import lax
from jax.experimental import pallas as pl
from jax.experimental.pallas import tpu as pltpu
from jax.sharding import PartitionSpec as P

HEADS = 16
EXP_DEV = 2
BF = jnp.bfloat16
F32 = jnp.float32
VMEM_BYTES = 56 * 1024 * 1024


def dot(a, b, ca, cb):
    return lax.dot_general(a, b, (((ca,), (cb,)), ((), ())), preferred_element_type=F32)


def exchange_kernel(
    inner, pieces, fused,
    q_ref, k_ref, v_ref, g_ref, hid_ref, routes_ref,
    out_ref, gq_ref, gk_ref, gv_ref, *rest,
):
    if fused:
        grad_ref, *rest = rest
        *rest, group, near_in, far_out, far_in, near_send, near_recv, far_send, far_recv = rest
    (
        cotg_ref, arr_ref, slots, own_state, peer_state, total_state, chain_in, chain_out, carried,
        score_ref, gscore_ref, cot_send, cot_recv, slot_send, slot_recv, st_send, st_recv,
        ch_send, ch_recv, local_sem,
    ) = rest
    count = lax.axis_size("seq")
    outer = count // inner
    me = lax.axis_index("seq")
    row = me // inner
    col = me % inner
    tokens = q_ref.shape[0]
    topk = hid_ref.shape[0]
    width = q_ref.shape[1]
    head = width // HEADS
    piece = width // pieces

    def remote(src, dst, send, recv, target, axis="seq"):
        return pltpu.make_async_remote_copy(
            src_ref=src, dst_ref=dst, send_sem=send, recv_sem=recv,
            device_id={axis: target}, device_id_type=pl.DeviceIdType.MESH,
        )

    if fused:
        grp = lax.axis_index("grp")
        chips = lax.axis_size("grp") // 2
        chip = grp // 2
        core = grp % 2
        sibling = chip * 2 + 1 - core
        far = [lax.rem(chip + off, chips) for off in range(1, chips)]

    barrier = pltpu.get_barrier_semaphore()

    def greet(step, carry):
        pl.semaphore_signal(
            barrier, inc=1, device_id={"seq": lax.rem(me + step, count)},
            device_id_type=pl.DeviceIdType.MESH,
        )
        return carry

    lax.fori_loop(1, count, greet, 0)
    greeted = count - 1
    if fused:
        for other in [sibling] + [x * 2 + core for x in far]:
            pl.semaphore_signal(
                barrier, inc=1, device_id={"grp": other}, device_id_type=pl.DeviceIdType.MESH
            )
        greeted += chips
    pl.semaphore_wait(barrier, greeted)

    def cot_at(c, origin):
        return cotg_ref.at[c, pl.ds(pl.multiple_of(origin * tokens, tokens), tokens), :]

    def own_piece(c):
        return g_ref.at[:, pl.ds(c * piece, piece)]

    def cot_copy(c, origin, src, lane, target):
        return remote(
            src, cot_at(c, origin), cot_send.at[c, origin, lane], cot_recv.at[c, origin], target
        )

    def cot_spread(c, origin, src, up, down, act):
        if up is not None:
            @pl.when(up)
            def _():
                act(cot_copy(c, origin, src, 0, me + inner))
        if down is not None:
            @pl.when(down)
            def _():
                act(cot_copy(c, origin, src, 1, me - inner))
        for off in range(1, inner):
            act(cot_copy(c, origin, src, 1 + off, row * inner + lax.rem(col + off, inner)))

    def cot_own(c, act):
        cot_spread(c, me, own_piece(c), row + 1 < outer, row >= 1, act)

    def cot_forward(c, step, act, wait):
        @pl.when(row >= step)
        def _():
            origin = me - step * inner
            if wait:
                cot_copy(c, origin, cot_at(c, origin), 0, origin).wait_recv()
            cot_spread(c, origin, cot_at(c, origin), row + 1 < outer, None, act)

        @pl.when(row + step < outer)
        def _():
            origin = me + step * inner
            if wait:
                cot_copy(c, origin, cot_at(c, origin), 0, origin).wait_recv()
            cot_spread(c, origin, cot_at(c, origin), None, row >= 1, act)

    start = lambda copy: copy.start()
    finish = lambda copy: copy.wait_send()

    for c in range(min(2, pieces)):
        cot_own(c, start)
    own_cot = [
        pltpu.make_async_copy(own_piece(c), cot_at(c, me), local_sem.at[1 + c])
        for c in range(pieces)
    ]
    for copy in own_cot:
        copy.start()

    position = me * tokens + lax.broadcasted_iota(jnp.int32, (tokens, 1), 0)
    scaling = lax.rsqrt((head * (position + 1)).astype(F32))
    causal = lax.broadcasted_iota(jnp.int32, (tokens, tokens), 0) >= lax.broadcasted_iota(
        jnp.int32, (tokens, tokens), 1
    )

    def heads_of(h):
        return pl.ds(pl.multiple_of(h * head, head), head)

    def states(h, carry):
        at = heads_of(h)
        q, k, v, g = q_ref[:, at], k_ref[:, at], v_ref[:, at], g_ref[:, at]
        own_state[0, at, :] = dot(k, v, 0, 0).astype(BF)
        own_state[1, at, :] = dot((q.astype(F32) * scaling).astype(BF), g, 0, 0).astype(BF)
        return carry

    lax.fori_loop(0, HEADS, states, 0)

    def state_copy(off):
        return remote(
            own_state, peer_state.at[col], st_send.at[off], st_recv.at[col],
            row * inner + lax.rem(col + off, inner),
        )

    for off in range(1, inner):
        state_copy(off).start()

    def fill(target):
        for x in range(EXP_DEV):
            expert = target * EXP_DEV + x
            total = None
            for j in range(topk):
                chosen = jnp.where(routes_ref[j : j + 1, :] == expert, 1.0, 0.0).astype(BF)
                term = hid_ref[j] * chosen
                total = term if total is None else total + term
            slots[target, x] = total

    def arr_at(source):
        return arr_ref.at[:, :, pl.ds(pl.multiple_of(source * tokens, tokens), tokens)]

    def slot_copy(off):
        target = lax.rem(me + off, count)
        return remote(
            slots.at[target], arr_at(me), slot_send.at[off], slot_recv.at[me], target,
        )

    def send_slots(off, carry):
        fill(lax.rem(me + off, count))
        slot_copy(off).start()
        return carry

    lax.fori_loop(1, count, send_slots, 0)
    fill(me)
    own_slots = pltpu.make_async_copy(slots.at[me], arr_at(me), local_sem.at[0])
    own_slots.start()

    def state_wait(off):
        source = lax.rem(col + off, inner)
        remote(
            own_state, peer_state.at[source], st_send.at[off], st_recv.at[source],
            row * inner + source,
        ).wait_recv()

    for off in range(1, inner):
        state_wait(off)
    peer_state[col] = own_state[...]

    def sum_rows(h, carry):
        at = heads_of(h)
        for which in range(2):
            total = jnp.zeros((head, head), F32)
            part = jnp.zeros((head, head), F32)
            for c in range(inner):
                block = peer_state[c, which, at, :].astype(F32)
                total = total + block
                counts = (c < col) if which == 0 else (c > col)
                part = part + jnp.where(counts, block, 0.0)
            total_state[which, at, :] = total
            carried[which, at, :] = part
        return carry

    lax.fori_loop(0, HEADS, sum_rows, 0)

    def chain_copy(which):
        target = me + inner if which == 0 else me - inner
        return remote(
            chain_out.at[which], chain_in.at[which], ch_send.at[which], ch_recv.at[which], target
        )

    def chain_step(which, first, last):
        if not first:
            chain_copy(which).wait_recv()

        def one(h, carry):
            at = heads_of(h)
            here = total_state[which, at, :]
            if not first:
                before = chain_in[which, at, :].astype(F32)
                carried[which, at, :] = carried[which, at, :] + before
                here = here + before
            if not last:
                chain_out[which, at, :] = here.astype(BF)
            return carry

        lax.fori_loop(0, HEADS, one, 0)
        if not last:
            chain_copy(which).start()

    def local_scores(h, carry):
        at = heads_of(h)
        q, k, v, g = q_ref[:, at], k_ref[:, at], v_ref[:, at], g_ref[:, at]
        score_ref[h] = jnp.where(causal, dot(q, k, 1, 1), 0.0).astype(BF)
        gscore_ref[h] = jnp.where(causal, dot(g, v, 1, 1), 0.0).astype(BF)
        return carry

    def advance(c, step):
        if step == 1 and c + 2 < pieces:
            cot_own(c + 2, start)
        cot_forward(c, step, start, True)

    events = [(c, step) for c in range(pieces) for step in range(1, outer)]
    for step in range(outer):
        @pl.when(row == step)
        def _():
            chain_step(0, step == 0, step == outer - 1)

        @pl.when(row == outer - 1 - step)
        def _():
            chain_step(1, step == 0, step == outer - 1)

        if step == 0:
            lax.fori_loop(0, HEADS, local_scores, 0)
        share = len(events) if step == outer - 1 else max(1, len(events) // (outer - step + 1))
        for event in events[:share]:
            advance(*event)
        events = events[share:]

    def finals(h, carry):
        at = heads_of(h)
        q, k, v, g = q_ref[:, at], k_ref[:, at], v_ref[:, at], g_ref[:, at]
        before = carried[0, at, :].astype(BF)
        after = carried[1, at, :].astype(BF)
        scores = score_ref[h]
        gscores = gscore_ref[h]
        weighted = (scores.astype(F32) * scaling).astype(BF)
        gweighted = (gscores.astype(F32) * scaling).astype(BF)
        out_ref[:, at] = ((dot(scores, v, 1, 0) + dot(q, before, 1, 0)) * scaling).astype(BF)
        gq_ref[:, at] = ((dot(gscores, k, 1, 0) + dot(g, before, 1, 1)) * scaling).astype(BF)
        gk_ref[:, at] = (dot(gweighted, q, 0, 0) + dot(v, after, 1, 1)).astype(BF)
        gv_ref[:, at] = (dot(weighted, g, 0, 0) + dot(k, after, 1, 0)).astype(BF)
        return carry

    lax.fori_loop(0, HEADS, finals, 0)

    def slots_last(off, carry):
        source = lax.rem(me + off, count)
        remote(
            slots.at[source], arr_at(source), slot_send.at[off], slot_recv.at[source], source
        ).wait_recv()
        slot_copy(off).wait_send()
        return carry

    lax.fori_loop(1, count, slots_last, 0)
    own_slots.wait()

    def near_copy(c, x):
        return remote(
            group.at[c, :, x * 2 + 1 - core], near_in.at[c, :, x],
            near_send.at[c, x], near_recv.at[c, x], sibling, "grp",
        )

    def far_copy(c, off):
        return remote(
            far_out.at[c, off], far_in.at[c, off], far_send.at[c, off], far_recv.at[c, off],
            far[off] * 2 + core, "grp",
        )

    def pair_sum(c, x, e):
        return group[c, e, x * 2 + core].astype(F32) + near_in[c, e, x].astype(F32)

    def multiply(c):
        quarter = group.shape[3]
        for e in range(EXP_DEV):
            term = dot(arr_ref[e], cotg_ref[c], 1, 0).astype(BF)
            for part in range(2 * chips):
                group[c, e, part] = term[part * quarter : (part + 1) * quarter]
        for x in range(chips):
            near_copy(c, x).start()

    def send_far(c):
        for x in range(chips):
            near_copy(c, x).wait()
        for off in range(chips - 1):
            for e in range(EXP_DEV):
                far_out[c, off, e] = pair_sum(c, far[off], e).astype(BF)
            far_copy(c, off).start()

    def close(c):
        for off in range(chips - 1):
            far_copy(c, off).wait()
        for e in range(EXP_DEV):
            total = pair_sum(c, chip, e)
            for off in range(chips - 1):
                total = total + far_in[c, off, e].astype(F32)
            grad_ref[e, :, pl.ds(c * piece, piece)] = total.astype(BF)

    for c in range(pieces):
        def cot_last(off, carry):
            source = lax.rem(col + off, inner)

            def one(line, carry):
                origin = line * inner + source
                cot_copy(c, origin, cot_at(c, origin), 0, row * inner + source).wait_recv()
                return carry

            return lax.fori_loop(0, outer, one, carry)

        lax.fori_loop(1, inner, cot_last, 0)
        own_cot[c].wait()
        if fused:
            multiply(c)
            if c >= 1:
                send_far(c - 1)
    if fused:
        send_far(pieces - 1)
        for c in range(pieces):
            close(c)

    for c in range(pieces):
        cot_own(c, finish)
        for step in range(1, outer):
            cot_forward(c, step, finish, False)
    for off in range(1, inner):
        state_copy(off).wait_send()

    @pl.when(row < outer - 1)
    def _():
        chain_copy(0).wait_send()

    @pl.when(row >= 1)
    def _():
        chain_copy(1).wait_send()


def exchange(query, key_in, value, cotangent, hidden, routes):
    count = lax.axis_size("seq")
    groups = lax.axis_size("grp")
    inner = 2 if count <= 8 else 8
    fused = count <= 8
    pieces = 4 if fused else 1
    tokens, width = query.shape
    head = width // HEADS
    units = hidden.shape[1]
    chips = groups // 2
    quarter = units // groups
    piece = width // pieces
    vmem = pl.BlockSpec(memory_space=pltpu.VMEM)
    anywhere = pl.BlockSpec(memory_space=pl.ANY)
    flat = jax.ShapeDtypeStruct((tokens, width), BF)
    dma = pltpu.SemaphoreType.DMA
    cot_shape = (pieces, count * tokens, piece)
    arr_shape = (EXP_DEV, units, count * tokens)
    scratch = [
        pltpu.VMEM((count, EXP_DEV, units, tokens), BF),
        pltpu.VMEM((2, width, head), BF),
        pltpu.VMEM((inner, 2, width, head), BF),
        pltpu.VMEM((2, width, head), F32),
        pltpu.VMEM((2, width, head), BF),
        pltpu.VMEM((2, width, head), BF),
        pltpu.VMEM((2, width, head), F32),
        pltpu.VMEM((HEADS, tokens, tokens), BF),
        pltpu.VMEM((HEADS, tokens, tokens), BF),
        dma((pieces, count, inner + 1)), dma((pieces, count)),
        dma((count,)), dma((count,)),
        dma((inner,)), dma((inner,)),
        dma((2,)), dma((2,)),
        dma((1 + pieces,)),
    ]
    if fused:
        out_shape = (flat,) * 4 + (jax.ShapeDtypeStruct((EXP_DEV, quarter, width), BF),)
        out_specs = (vmem,) * 5
        far = (pieces, chips - 1, EXP_DEV, quarter, piece)
        scratch = [pltpu.VMEM(cot_shape, BF), pltpu.VMEM(arr_shape, BF)] + scratch + [
            pltpu.VMEM((pieces, EXP_DEV, groups, quarter, piece), BF),
            pltpu.VMEM((pieces, EXP_DEV, chips, quarter, piece), BF),
            pltpu.VMEM(far, BF), pltpu.VMEM(far, BF),
            dma((pieces, chips)), dma((pieces, chips)),
            dma((pieces, chips - 1)), dma((pieces, chips - 1)),
        ]
    else:
        out_shape = (flat,) * 4 + (
            jax.ShapeDtypeStruct(cot_shape, BF), jax.ShapeDtypeStruct(arr_shape, BF)
        )
        out_specs = (vmem,) * 4 + (anywhere,) * 2
    result = pl.pallas_call(
        functools.partial(exchange_kernel, inner, pieces, fused),
        out_shape=out_shape,
        in_specs=[vmem] * 6,
        out_specs=out_specs,
        scratch_shapes=scratch,
        compiler_params=pltpu.CompilerParams(
            collective_id=0, has_side_effects=True, vmem_limit_bytes=VMEM_BYTES
        ),
        name="exchange",
    )(query, key_in, value, cotangent, hidden, routes)
    if fused:
        return result
    *heads, all_cot, arrived = result
    term = jnp.einsum("xft,td->xfd", arrived, all_cot[0], preferred_element_type=F32)
    expert_grad = lax.psum_scatter(term.astype(BF), "grp", scatter_dimension=1, tiled=True)
    return (*heads, expert_grad)


def per_device(query, key_in, value, cotangent, routes, gates, hidden):
    scaled = (gates[0][:, :, None] * hidden[0].astype(F32)).astype(BF).transpose(1, 2, 0)
    outputs, grad_q, grad_k, grad_v, expert_grad = exchange(
        query[0], key_in[0], value[0], cotangent[0], scaled, routes[0].T
    )
    return (outputs[None], grad_q[None], grad_k[None], grad_v[None], expert_grad)


def solution(mesh):
    rows = P("grp", "seq", None)
    in_specs = (rows, rows, rows, rows, rows, rows, P("grp", "seq", None, None))
    out_specs = (rows, rows, rows, rows, P("seq", "grp", None))
    return jax.shard_map(
        per_device, mesh=mesh, in_specs=in_specs, out_specs=out_specs, check_vma=False
    )
```

time: 224 us -> 177 us (0.79)
  waiting for transfers between devices: 55.1 us -> 0 us
  Pallas kernels: 135 us -> 165 us
  between operations: 14.1 us -> 0.66 us
  matrix products: 10.7 us -> 0 us
    reduce_scatter x1 -> x0, waiting for transfers between devices: 55.1 us -> none  [per_device(): lax.psum_scatter(group_term.astype(BF), 'grp', scatter_dimension=1, tiled...]
    pallas_call x1, Pallas kernels: 135 us -> 165 us  [exchange(): pl.pallas_call(functools.partial(exchange_kernel, inner, pieces, fused),...]
    dot_general x1 -> x0, matrix products: 10.7 us -> none  [per_device(): jnp.einsum('xtf,td->xfd', arrived, all_cot, preferred_element_type=F32)]
    unnamed x15 -> x13, local copies, waits for them, and re-layouts: 6.84 us -> 8.62 us
  transfers between devices with their start and end apart: 1 -> 0, of which waited for: 1 -> 0; matrix products, arithmetic and copies ran while one was open for 0% -> 0% of each run, Pallas kernels for 0% -> 0%
where the time goes in v2:
time: 177 us; the launch traced here: 176 us
  Pallas kernels  165 us (93%)
  local copies, waits for them, and re-layouts  8.62 us (5%)
  other arithmetic  2.43 us (1%)
    pallas_call x1, Pallas kernels, exchange(): pl.pallas_call(functools.partial(exchange_kernel, inner, pieces, fused),...  165 us
    unnamed x13, local copies, waits for them, and re-layouts  8.62 us

profile of v2, /device:TPU:0, one launch (start us, length us, event | category | flops | bytes accessed | tf_op | source)
XLA Modules:
  0.0 176.4 jit_solution(2720898063692846367)
XLA Ops:
  0.6 1.3 copy.16
  1.9 0.7 copy.17
  2.6 2.4 %fusion.1.hid_ref = bf16[6,704,128]{2,1,0:T(8,128)(2,1)} fusion(bf16[1,128,6,704]{1,3,2,0:T(8,128)(2,1)} %param.13, f32[128,6]{0,1:T(8,128)S(1)} %bitcast.30), kind=kLoop, calls=%fused_computation.2 | loop fusion | flops 1622016 | bytes 2165760 | tf_op jit(solution)/shard_map/transpose | solution.py:445
  5.0 164.7 %exchange.1 = (bf16[128,2048]{1,0:T(8,128)(2,1)}, bf16[128,2048]{1,0:T(8,128)(2,1)}, bf16[128,2048]{1,0:T(8,128)(2,1)}, bf16[128,2048]{1,0:T(8,128)(2,1)}, bf16[2,176,2048]{2,1,0:T(8,128)(2,1)}) custom-call(bf16[128,2048]{1,0:T(8,128)(2,1)} %bitcast.21, bf16[128,2048]{1,0:T(8,128)(2,1)} %bitcast.22, bf16[128,2048]{1,0:T(8,128)(2,1)} %bitcast.23, ...), custom_call_target="tpu_custom_call" | custom-call | tf_op jit(solution)/shard_map/exchange/pallas_call | solution.py:425
  169.7 0.0 copy-start.2
  169.7 0.0 copy-start.1
  169.7 2.0 %copy.23 = bf16[1,128,2048]{2,1,0:T(8,128)(2,1)} copy(bf16[1,128,2048]{2,1,0:T(8,128)(2,1)} %bitcast.28) | data formatting | bytes 1048576
  171.7 0.0 copy-start
  171.7 2.0 %copy.24 = bf16[1,128,2048]{2,1,0:T(8,128)(2,1)} copy(bf16[1,128,2048]{2,1,0:T(8,128)(2,1)} %bitcast.27) | data formatting | bytes 1048576
  173.7 0.0 copy-done.2
  173.7 0.8 copy.25
  174.5 0.0 copy-done.1
  174.5 0.8 copy.26
  175.3 0.0 copy-done
  175.3 1.1 copy.27
Async XLA Ops:
  169.7 4.0 %copy-start.2 = (bf16[128,2048]{1,0:T(8,128)(2,1)S(1)}, bf16[128,2048]{1,0:T(8,128)(2,1)}, u32[]{:S(2)}) copy-start(bf16[128,2048]{1,0:T(8,128)(2,1)} %get-tuple-element.12) | copy-start | bytes 1572868
  169.7 4.8 %copy-start.1 = (bf16[128,2048]{1,0:T(8,128)(2,1)S(1)}, bf16[128,2048]{1,0:T(8,128)(2,1)}, u32[]{:S(2)}) copy-start(bf16[128,2048]{1,0:T(8,128)(2,1)} %get-tuple-element.13) | copy-start | bytes 1572868
  171.7 3.6 %copy-start = (bf16[2,176,2048]{2,1,0:T(8,128)(2,1)S(1)}, bf16[2,176,2048]{2,1,0:T(8,128)(2,1)}, u32[]{:S(2)}) copy-start(bf16[2,176,2048]{2,1,0:T(8,128)(2,1)} %get-tuple-element.24) | copy-start | bytes 4325380
